TPU v7x, 32 devices: a whole 2x2x4 slice. The times are simulated.
32 devices in a mesh: grp: 4 (over z), seq: 8 (over y, x, core).
Axes of the slice: x: 2, y: 2, z: 4, core: 2. Of those that a mesh axis runs over, the one named last changes fastest.
Arguments:
- queries: bfloat16 [4, 4, 2, 128, 576], P('grp', None, None, 'seq'), may hold values from -1024 to 1024
- latent_cache: bfloat16 [4, 65536, 576], P(None, ('grp', 'seq')), may hold values from -6 to 6
- lengths: int32 [4], replicated, may hold values from 8192 to 65536
- owner_group: int32 [4], replicated, may hold values from 0 to 3, as said below
Outputs:
- attended: bfloat16 [4, 2, 128, 512], P(None, None, ('grp', 'seq'))
Inputs may be any that keep to these rules, and one draw needn't show every extreme that they name: `owner_group`: each of 0 to 3 appears exactly once.
All inputs are finite; a program needn't handle non-finite values.
Results may differ from a plain program's by a relative error of at most 0.0015.
Values may be sent and summed in bfloat16 or wider, within the bound.
A program may use at most 64 MiB of HBM per device.

v0:
```python
import jax
import jax.numpy as jnp
from jax import lax
from jax.sharding import PartitionSpec as P

LATENT_WIDTH = 512


softmax_scale = 192.0 ** (-0.5)
masked_score = -1e30


def block_partial(query_matrix, cache_block, limits, block_rank, blocks):
    batch, rows, width = query_matrix.shape
    slots = cache_block.shape[1]
    stripe = slots // 2
    drafts = limits.shape[1]
    heads = rows // drafts
    offset = jnp.arange(slots, dtype=jnp.int32)
    position = jnp.where(
        offset < stripe,
        block_rank * stripe + offset,
        (2 * blocks - 1 - block_rank) * stripe + offset - stripe,
    )
    valid_slot = position[None, None, :] < limits[:, :, None]
    logit_scores = (
        jnp.einsum("fdi,fei->fde", query_matrix, cache_block, preferred_element_type=jnp.float32)
        * softmax_scale
    )
    logit_scores = logit_scores.reshape(batch, drafts, heads, slots)
    logit_scores = jnp.where(valid_slot[:, :, None, :], logit_scores, masked_score)
    local_max = jnp.max(logit_scores, axis=3)
    weights = jnp.where(
        valid_slot[:, :, None, :], jnp.exp(logit_scores - local_max[..., None]), 0.0
    )
    local_sum = jnp.sum(weights, axis=3)
    rounded_values = weights.astype(jnp.bfloat16).reshape(batch, rows, slots)
    partial_output = jnp.einsum(
        "giv,gvu->giu",
        rounded_values,
        cache_block[:, :, :LATENT_WIDTH],
        preferred_element_type=jnp.float32,
    )
    return (local_max, local_sum, partial_output.reshape(batch, drafts, heads, LATENT_WIDTH))


def owned_rows(copies, owner_group, group_count, group_rank):
    batch, drafts = (copies.shape[1], copies.shape[2])
    row_index = jnp.arange(batch * drafts, dtype=jnp.int32) % group_count
    owners = jnp.take(owner_group, row_index).reshape(batch, drafts)
    mine = owners == group_rank
    return jnp.where(mine[None, :, :, None, None], copies.astype(jnp.float32), 0.0)


def shards(queries, latent_cache, lengths, owner_group):
    seq_count = lax.axis_size("seq")
    group_count = lax.axis_size("grp")
    blocks = seq_count * group_count
    group_rank = lax.axis_index("grp")
    device_rank = group_rank * seq_count + lax.axis_index("seq")
    kept = owned_rows(queries, owner_group, group_count, group_rank)
    own_heads = lax.psum(kept.astype(jnp.bfloat16), "grp")
    gathered = lax.all_gather(own_heads, "seq", axis=3, tiled=True)
    batch, drafts, heads, width = gathered.shape[1:]
    query_matrix = gathered.reshape(batch, drafts * heads, width)
    limits = lengths[:, None] - drafts + 1 + jnp.arange(drafts, dtype=jnp.int32)[None, :]
    local_parts = block_partial(query_matrix, latent_cache, limits, device_rank, blocks)
    local_max, local_sum, partial_output = local_parts
    highest = lax.pmax(local_max, ("grp", "seq"))
    factor = jnp.exp(local_max - highest)
    total, summed = (
        lax.psum_scatter(local_sum * factor, ("grp", "seq"), scatter_dimension=2, tiled=True),
        lax.psum_scatter(
            partial_output * factor[..., None], ("grp", "seq"), scatter_dimension=2, tiled=True
        ),
    )
    return (summed / total[..., None]).astype(jnp.bfloat16)


def solution(mesh):
    return jax.shard_map(
        shards,
        mesh=mesh,
        in_specs=(P("grp", None, None, "seq", None), P(None, ("grp", "seq"), None), P(), P()),
        out_specs=P(None, None, ("grp", "seq"), None),
        check_vma=False,
    )
```

profile of v0, /device:TPU:0, one launch (start us, length us, event | category | flops | bytes accessed | tf_op | source)
XLA Modules:
  0.0 275.0 jit_solution(3038373703724209350)
XLA Ops:
  6.5 0.0 copy-start
  6.5 0.0 all-reduce.5.cloned.1.call-start
  6.6 0.6 copy-done
  7.2 0.6 gather_fusion
  7.8 0.1 gather.7
  7.9 1.7 select_convert_fusion
  9.6 0.0 all-reduce.5.cloned.1.call-update
  9.6 0.0 all-gather.2.cloned.1.call-start
  9.7 37.4 %all-reduce.5.cloned.1.call-done = bf16[1,4,2,16,576]{4,3,2,1,0:T(8,128)(2,1)} async-done(((bf16[1,4,2,16,576]{4,3,2,1,0:T(8,128)(2,1)}), bf16[1,4,2,16,576]{4,3,2,1,0:T(8,128)(2,1)}) %all-reduce.5.cloned.1.call-update) | async-done | bytes 147472 | tf_op jit(solution)/shard_map/psum | solution.py:62
  47.1 0.0 all-gather.2.cloned.1.call-update
  47.1 0.0 all-reduce.7.cloned.1.call-start
  47.2 0.7 broadcast_add_fusion
  47.9 0.1 iota_add_fusion
  47.9 0.1 broadcast_compare_fusion
  48.0 25.5 %all-gather.2.cloned.1.call-done = bf16[1,4,2,128,576]{4,3,2,1,0:T(8,128)(2,1)} async-done(((bf16[1,4,2,16,576]{4,3,2,1,0:T(8,128)(2,1)}), bf16[1,4,2,128,576]{4,3,2,1,0:T(8,128)(2,1)}) %all-gather.2.cloned.1.call-update) | async-done | bytes 1179664 | tf_op jit(solution)/shard_map/all_gather | solution.py:63
  73.5 6.7 %fusion.2 = (f32[4,256]{1,0:T(4,128)S(1)}, f32[4,256,2048]{2,1,0:T(8,128)S(1)}) fusion(pred[4,2,2048]{2,1,0:T(4,128)(4,1)S(1)} %broadcast_compare_fusion, bf16[4,256,576]{2,1,0:T(8,128)(2,1)} %bitcast.30, bf16[4,2048,576]{1,2,0:T(8,128)(2,1)} %param.5), kind=kOutput, calls=%fused_computation.5 | convolution fusion | flops 2422209536 | bytes 19025920 | tf_op jit(solution)/shard_map/fdi,fei->fde/dot_general | solution.py:27
  80.2 3.9 %fusion.3 = (f32[4,256]{1,0:T(4,128)S(1)}, bf16[4,256,2048]{2,1,0:T(8,128)(2,1)}) fusion(f32[4,256,2048]{2,1,0:T(8,128)S(1)} %get-tuple-element.10, f32[4,256]{1,0:T(4,128)S(1)} %get-tuple-element.9, pred[4,2,2048]{2,1,0:T(4,128)(4,1)S(1)} %broadcast_compare_fusion), kind=kLoop, calls=%fused_computation.6 | loop fusion | flops 12581888 | bytes 12607488 | tf_op jit(solution)/shard_map/reduce_sum | solution.py:36
  84.1 39.3 %pmax.7 = f32[4,2,128]{2,0,1:T(4,128)S(1)} all-reduce(f32[4,2,128]{2,0,1:T(4,128)S(1)} %bitcast.31), channel_id=1, replica_groups=mesh['grp'=4,'seq'=8] {'grp','seq'}, use_global_device_ids=true, to_apply=%region_2.3 | all-reduce | flops 1024 | bytes 8192 | tf_op jit(solution)/shard_map/pmax | solution.py:69
  123.4 7.0 %fusion = f32[4,256,512]{2,1,0:T(8,128)S(1)} fusion(bf16[4,256,2048]{2,1,0:T(8,128)(2,1)} %get-tuple-element.8, bf16[4,2048,576]{1,2,0:T(8,128)(2,1)} %param.5), kind=kOutput, calls=%fused_computation.3 | convolution fusion | flops 2147483648 | bytes 14680064 | tf_op jit(solution)/shard_map/giv,gvu->giu/dot_general | solution.py:38
  130.4 1.5 broadcast_multiply_fusion
  131.9 0.0 all-reduce.7.cloned.1.call-update
  132.0 41.4 %all-reduce.1 = f32[4,2,128]{2,0,1:T(4,128)S(1)} all-reduce(f32[4,2,128]{2,0,1:T(4,128)S(1)} %get-tuple-element.5), channel_id=3, replica_groups=mesh['grp'=4,'seq'=8] {'grp','seq'}, use_global_device_ids=true, to_apply=%region_5.6.clone | all-reduce | flops 1024 | bytes 8192
  173.3 0.1 constant_dynamic-slice_fusion
  173.4 93.5 %all-reduce.7.cloned.1.call-done = f32[4,2,128,512]{3,2,1,0:T(8,128)} async-done(((f32[4,2,128,512]{3,2,1,0:T(8,128)}), f32[4,2,128,512]{3,2,1,0:T(8,128)}) %all-reduce.7.cloned.1.call-update) | async-done | bytes 2097168
  266.9 1.6 fusion.5
  (7 shorter events, 0.1 us)
Async XLA Ops:
  6.5 0.7 copy-start
  6.5 40.6 %all-reduce.5.cloned.1.call-start = ((), (), s32[]{:S(2)}) async-start(), calls=%async_computation | async-start | bytes 327680 | tf_op jit(solution)/shard_map/psum | solution.py:62
  9.6 63.9 %all-gather.2.cloned.1.call-start = ((), (), s32[]{:S(2)}) async-start(), calls=%async_computation.1 | async-start | bytes 1474560 | tf_op jit(solution)/shard_map/all_gather | solution.py:63
  47.1 219.8 %all-reduce.7.cloned.1.call-start = ((), (), s32[]{:S(2)}) async-start(), calls=%async_computation.2 | async-start | bytes 4194304
Sparse Core Ops, SparseCore 0:
  9.8 37.3 all-reduce.4
  49.2 24.3 all-gather.1
  132.1 134.7 all-reduce.6
where the time goes:
time: 276 us; the launch traced here: 275 us
  waiting for transfers between devices  156 us (57%)
  blocking collectives  80.7 us (29%)
  matrix products  13.7 us (5%)
  between operations  13.2 us (5%)
  other arithmetic  9.53 us (3%)
    unnamed x4, waiting for transfers between devices  93.5 us
    unnamed x1, blocking collectives  41.4 us
    pmax x1, blocking collectives, shards(): highest = lax.pmax(local_max, ('grp', 'seq'))  39.3 us
    psum x1, waiting for transfers between devices, shards(): own_heads = lax.psum(kept.astype(jnp.bfloat16), 'grp')  37.4 us
    all_gather x1, waiting for transfers between devices, shards(): gathered = lax.all_gather(own_heads, 'seq', axis=3, tiled=True)  25.5 us
    dot_general x1, matrix products, block_partial(): jnp.einsum('giv,gvu->giu', rounded_values, cache_block[:, :, :LATENT_WIDT...  7.03 us
    dot_general x1, matrix products, block_partial(): jnp.einsum('fdi,fei->fde', query_matrix, cache_block, preferred_element_t...  6.67 us
  transfers between devices with their start and end apart: 3, of which 3 were waited for; matrix products, arithmetic and copies ran while one was open for 0% of the time, Pallas kernels for 0%

commit v1 on v0

--- a/solution.py
+++ b/solution.py
@@ -1,13 +1,325 @@
+import functools
+
 import jax
 import jax.numpy as jnp
+import numpy as np
 from jax import lax
+from jax.experimental import pallas as pl
+from jax.experimental.pallas import tpu as pltpu
 from jax.sharding import PartitionSpec as P
 
 LATENT_WIDTH = 512
+LOG2E = 1.4426950408889634
+MESH = pl.DeviceIdType.MESH
+TAIL = 128
 
 
 softmax_scale = 192.0 ** (-0.5)
 masked_score = -1e30
+
+
+def merge(parts, latent):
+    tops = [part[..., latent + TAIL // 2 : latent + TAIL // 2 + 1] for part in parts]
+    top = functools.reduce(jnp.maximum, tops)
+    total, output = None, None
+    for part, own_top in zip(parts, tops):
+        factor = jnp.exp2(own_top - top)
+        part_sum = part[..., latent : latent + 1] * factor
+        part_output = part[..., :latent] * factor
+        total = part_sum if total is None else total + part_sum
+        output = part_output if output is None else output + part_output
+    return top, total, output
+
+
+def pack_tail(top, total):
+    shape = top.shape[:-1] + (TAIL,)
+    lane = lax.broadcasted_iota(jnp.int32, shape, len(shape) - 1)
+    return jnp.where(
+        lane < TAIL // 2, jnp.broadcast_to(total, shape), jnp.broadcast_to(top, shape)
+    )
+
+
+def fused_kernel(dims, lengths_ref, owner_ref, query_ref, order_ref, cache_ref, out_ref, *scratch):
+    batch, drafts, groups, seqs, chunks, heads_per, slots, width, latent = dims
+    chips = seqs // 2
+    per_chunk = batch // chunks
+    rows_per = drafts * heads_per
+    rows = drafts * heads_per * groups * seqs
+    gathered = scratch[:chunks]
+    (cache, query, packed, core_in, plane_out, plane_in, group_out, group_in) = scratch[
+        chunks : chunks + 8
+    ]
+    (
+        cache_sem,
+        zq_send, zq_recv, pq_send, pq_recv, sq_send, sq_recv,
+        c_send, c_recv, p_send, p_recv, z_send, z_recv,
+    ) = scratch[chunks + 8 :]
+
+    grp = lax.axis_index("grp")
+    seq = lax.axis_index("seq")
+    core = lax.rem(seq, 2)
+    chip = seq // 2
+    sibling = seq + 1 - 2 * core
+
+    def group_peer(step):
+        return lax.rem(grp + step, groups)
+
+    def chip_peer(step):
+        return lax.rem(chip + step, chips)
+
+    def cache_copy(b):
+        return pltpu.make_async_copy(cache_ref.at[b], cache.at[b], cache_sem.at[b])
+
+    for b in range(batch):
+        cache_copy(b).start()
+
+    peers = [(group_peer(k), seq) for k in range(1, groups)]
+    peers += [(grp, chip_peer(k) * 2 + core) for k in range(1, chips)]
+    peers += [(grp, sibling)]
+    barrier = pltpu.get_barrier_semaphore()
+    for peer in peers:
+        pl.semaphore_signal(barrier, inc=1, device_id=peer, device_id_type=MESH)
+
+    held = jnp.int32(0)
+    for k in range(groups):
+        held = jnp.where(owner_ref[k] == grp, k, held)
+    for n in range(chunks):
+        gathered[n][seq, grp] = query_ref[n, held]
+    pl.semaphore_wait(barrier, len(peers))
+
+    def remote(src, dst, send, recv, peer):
+        return pltpu.make_async_remote_copy(
+            src_ref=src, dst_ref=dst, send_sem=send, recv_sem=recv,
+            device_id=peer, device_id_type=MESH,
+        )
+
+    def zq(n, k):
+        ref = gathered[n].at[seq, grp]
+        return remote(ref, ref, zq_send.at[n, k - 1], zq_recv.at[n, k - 1], (group_peer(k), seq))
+
+    def pq(n, k):
+        ref = gathered[n].at[seq]
+        return remote(
+            ref, ref, pq_send.at[n, k - 1], pq_recv.at[n, k - 1], (grp, chip_peer(k) * 2 + core)
+        )
+
+    def sq(n, k):
+        ref = gathered[n].at[chip_peer(chips - k) * 2 + core]
+        return remote(ref, ref, sq_send.at[n, k], sq_recv.at[n, k], (grp, sibling))
+
+    def c_copy(b):
+        return remote(
+            packed.at[b, 1 - core], core_in.at[b], c_send.at[b], c_recv.at[b], (grp, sibling)
+        )
+
+    def p_copy(b, k):
+        return remote(
+            plane_out.at[b, chip_peer(k)], plane_in.at[b, k - 1],
+            p_send.at[b, k - 1], p_recv.at[b, k - 1], (grp, chip_peer(k) * 2 + core),
+        )
+
+    def z_copy(b, k):
+        return remote(
+            group_out.at[b, group_peer(k)], group_in.at[b, k - 1],
+            z_send.at[b, k - 1], z_recv.at[b, k - 1], (group_peer(k), seq),
+        )
+
+    def forward(n):
+        for k in range(1, chips):
+            pq(n, k).wait_recv()
+            sq(n, k).start()
+
+    for n in range(chunks):
+        for k in range(1, groups):
+            zq(n, k).start()
+    for n in range(chunks):
+        for k in range(1, groups):
+            zq(n, k).wait_recv()
+        for k in range(1, chips):
+            pq(n, k).start()
+        sq(n, 0).start()
+    forward(0)
+
+    blocks = groups * seqs
+    rank = grp * seqs + seq
+    stripe = slots // 2
+    log_scale = softmax_scale * LOG2E
+
+    def step(b, carry):
+        @pl.when(b < batch)
+        def _():
+            for n in range(chunks):
+                @pl.when(b == n * per_chunk)
+                def _():
+                    for k in range(chips):
+                        sq(n, k).wait_recv()
+
+                @pl.when(b // per_chunk == n)
+                def _():
+                    whole = []
+                    for t in range(drafts):
+                        row = b * drafts + t
+                        owner = owner_ref[lax.rem(row, groups)]
+                        whole.append(gathered[n][:, owner].reshape(rows // drafts, width))
+                    stacked = jnp.concatenate(whole, axis=0)
+                    query[...] = jnp.dot(
+                        order_ref[...], stacked, preferred_element_type=jnp.float32
+                    ).astype(jnp.bfloat16)
+
+            cache_copy(b).wait()
+            scores = lax.dot_general(
+                query[...], cache[b], (((1,), (1,)), ((), ())),
+                preferred_element_type=jnp.float32,
+            )
+            offset = lax.broadcasted_iota(jnp.int32, (1, slots), 1)
+            position = jnp.where(
+                offset < stripe,
+                rank * stripe + offset,
+                (2 * blocks - 1 - rank) * stripe + offset - stripe,
+            )
+            row_index = lax.broadcasted_iota(jnp.int32, (rows, 1), 0)
+            draft = lax.rem(row_index, rows_per) // heads_per
+            limit = lengths_ref[b] - drafts + 1 + draft
+            scores = jnp.where(position < limit, scores, masked_score)
+            top = jnp.maximum(jnp.max(scores, axis=1, keepdims=True), 0.1 * masked_score)
+            weights = jnp.exp2((scores - top) * log_scale)
+            total = jnp.sum(weights, axis=1, keepdims=True)
+            output = jnp.dot(
+                weights.astype(jnp.bfloat16), cache[b, :, :latent],
+                preferred_element_type=jnp.float32,
+            )
+            split = (2, chips, groups * rows_per)
+            packed[b, :, :, :, :latent] = output.reshape(split + (latent,))
+            packed[b, :, :, :, latent:] = pack_tail(top * log_scale, total).reshape(split + (TAIL,))
+            c_copy(b).start()
+
+            for n in range(1, chunks):
+                @pl.when(b == n * per_chunk - 1)
+                def _():
+                    forward(n)
+
+        @pl.when((b >= 1) & (b < batch + 1))
+        def _():
+            at = b - 1
+            c_copy(at).wait_recv()
+            top, total, output = merge([packed[at, core], core_in[at]], latent)
+            plane_out[at, :, :, :latent] = output
+            plane_out[at, :, :, latent:] = pack_tail(top, total)
+            for k in range(1, chips):
+                p_copy(at, k).start()
+
+        @pl.when((b >= 2) & (b < batch + 2))
+        def _():
+            at = b - 2
+            for k in range(1, chips):
+                p_copy(at, k).wait_recv()
+            parts = [plane_out[at, chip]] + [plane_in[at, k] for k in range(chips - 1)]
+            top, total, output = merge(parts, latent)
+            group_out[at, :, :, :latent] = output.reshape(groups, rows_per, latent)
+            group_out[at, :, :, latent:] = pack_tail(top, total).reshape(groups, rows_per, TAIL)
+            for k in range(1, groups):
+                z_copy(at, k).start()
+
+        @pl.when(b >= 3)
+        def _():
+            at = b - 3
+            for k in range(1, groups):
+                z_copy(at, k).wait_recv()
+            parts = [group_out[at, grp]] + [group_in[at, k] for k in range(groups - 1)]
+            top, total, output = merge(parts, latent)
+            out_ref[at] = output / total
+            c_copy(at).wait_send()
+            for k in range(1, chips):
+                p_copy(at, k).wait_send()
+            for k in range(1, groups):
+                z_copy(at, k).wait_send()
+
+        return carry
+
+    lax.fori_loop(0, batch + 3, step, 0)
+    for n in range(chunks):
+        for k in range(1, groups):
+            zq(n, k).wait_send()
+        for k in range(1, chips):
+            pq(n, k).wait_send()
+        for k in range(chips):
+            sq(n, k).wait_send()
+
+
+def row_order(drafts, groups, seqs, heads_per):
+    heads = groups * seqs * heads_per
+    source = np.arange(drafts * heads).reshape(drafts, groups, seqs // 2, 2, heads_per)
+    source = source.transpose(3, 2, 1, 0, 4).reshape(-1)
+    return (source[:, None] == np.arange(drafts * heads)[None, :]).astype(np.float32)
+
+
+def fused_shards(queries, latent_cache, lengths, owner_group):
+    seqs = lax.axis_size("seq")
+    groups = lax.axis_size("grp")
+    _, batch, drafts, part_heads, width = queries.shape
+    slots = latent_cache.shape[1]
+    latent = LATENT_WIDTH
+    heads_per = part_heads // groups
+    chunks = batch * drafts // groups
+    chips = seqs // 2
+    rows_per = drafts * heads_per
+    rows = rows_per * groups * seqs
+    dims = (batch, drafts, groups, seqs, chunks, heads_per, slots, width, latent)
+    wide = latent + TAIL
+    order = jnp.asarray(row_order(drafts, groups, seqs, heads_per), jnp.bfloat16)
+    f32, bf16 = jnp.float32, jnp.bfloat16
+    dma = pltpu.SemaphoreType.DMA
+    out = pl.pallas_call(
+        functools.partial(fused_kernel, dims),
+        out_shape=jax.ShapeDtypeStruct((batch, rows_per, latent), f32),
+        in_specs=[
+            pl.BlockSpec(memory_space=pltpu.SMEM),
+            pl.BlockSpec(memory_space=pltpu.SMEM),
+            pl.BlockSpec(memory_space=pltpu.VMEM),
+            pl.BlockSpec(memory_space=pltpu.VMEM),
+            pl.BlockSpec(memory_space=pl.ANY),
+        ],
+        out_specs=pl.BlockSpec(memory_space=pltpu.VMEM),
+        scratch_shapes=[pltpu.VMEM((seqs, groups, part_heads, width), bf16)] * chunks
+        + [
+            pltpu.VMEM((batch, slots, width), bf16),
+            pltpu.VMEM((rows, width), bf16),
+            pltpu.VMEM((batch, 2, chips, groups * rows_per, wide), f32),
+            pltpu.VMEM((batch, chips, groups * rows_per, wide), f32),
+            pltpu.VMEM((batch, chips, groups * rows_per, wide), f32),
+            pltpu.VMEM((batch, chips - 1, groups * rows_per, wide), f32),
+            pltpu.VMEM((batch, groups, rows_per, wide), f32),
+            pltpu.VMEM((batch, groups - 1, rows_per, wide), f32),
+            dma((batch,)),
+            dma((chunks, groups - 1)), dma((chunks, groups - 1)),
+            dma((chunks, chips - 1)), dma((chunks, chips - 1)),
+            dma((chunks, chips)), dma((chunks, chips)),
+            dma((batch,)), dma((batch,)),
+            dma((batch, chips - 1)), dma((batch, chips - 1)),
+            dma((batch, groups - 1)), dma((batch, groups - 1)),
+        ],
+        compiler_params=pltpu.CompilerParams(
+            collective_id=0, has_side_effects=True, vmem_limit_bytes=48 * 1024 * 1024
+        ),
+    )(lengths, owner_group, queries.reshape(chunks, groups, part_heads, width), order, latent_cache)
+    return out.reshape(batch, drafts, heads_per, latent).astype(bf16)
+
+
+def fits_kernel(mesh):
+    seqs, groups = mesh.shape["seq"], mesh.shape["grp"]
+
+    def check(queries):
+        _, batch, drafts, heads, _ = queries.shape
+        parts = seqs * groups
+        rows = batch * drafts
+        return (
+            seqs % 2 == 0 and seqs > 2 and groups > 1
+            and heads % parts == 0 and (heads // parts * drafts) % 8 == 0
+            and (heads // seqs) % 16 == 0
+            and rows % groups == 0 and batch % (rows // groups) == 0
+        )
+
+    return check
 
 
 def block_partial(query_matrix, cache_block, limits, block_rank, blocks):
@@ -78,10 +390,15 @@
 
 
 def solution(mesh):
-    return jax.shard_map(
-        shards,
-        mesh=mesh,
-        in_specs=(P("grp", None, None, "seq", None), P(None, ("grp", "seq"), None), P(), P()),
-        out_specs=P(None, None, ("grp", "seq"), None),
-        check_vma=False,
-    )
+    check = fits_kernel(mesh)
+
+    def attend(queries, latent_cache, lengths, owner_group):
+        return jax.shard_map(
+            fused_shards if check(queries) else shards,
+            mesh=mesh,
+            in_specs=(P("grp", None, None, "seq", None), P(None, ("grp", "seq"), None), P(), P()),
+            out_specs=P(None, None, ("grp", "seq"), None),
+            check_vma=False,
+        )(queries, latent_cache, lengths, owner_group)
+
+    return attend

time: 276 us -> 60 us (0.22)
  waiting for transfers between devices: 156 us -> 0 us
  blocking collectives: 80.7 us -> 0 us
  Pallas kernels: 0 us -> 44.7 us
  matrix products: 13.7 us -> 0 us
  local copies, waits for them, and re-layouts: 1.45 us -> 14.8 us
  between operations: 13.2 us -> 0.03 us
  other arithmetic: 9.53 us -> 0.01 us
    unnamed x4 -> x0, waiting for transfers between devices: 93.5 us -> none
    pallas_call x0 -> x1, Pallas kernels: none -> 44.7 us  [fused_shards(): pl.pallas_call(functools.partial(fused_kernel, dims), out_shape=jax.Shape...]
    unnamed x1 -> x0, blocking collectives: 41.4 us -> none
    pmax x1 -> x0, blocking collectives: 39.3 us -> none  [shards(): highest = lax.pmax(local_max, ('grp', 'seq'))]
    psum x1 -> x0, waiting for transfers between devices: 37.4 us -> none  [shards(): own_heads = lax.psum(kept.astype(jnp.bfloat16), 'grp')]
    all_gather x1 -> x0, waiting for transfers between devices: 25.5 us -> none  [shards(): gathered = lax.all_gather(own_heads, 'seq', axis=3, tiled=True)]
    dot_general x2 -> x0, matrix products: 13.7 us -> none  [the longest x1 7.03 us: block_partial(): jnp.einsum('giv,gvu->giu', rounded_values, cache_block[:, :, :LATENT_WIDT...]
    unnamed x3 -> x9, local copies, waits for them, and re-layouts: 0.71 us -> 14.2 us
  transfers between devices with their start and end apart: 3 -> 0, of which waited for: 3 -> 0; matrix products, arithmetic and copies ran while one was open for 0% -> 0% of each run, Pallas kernels for 0% -> 0%
where the time goes in v1:
time: 60 us; the launch traced here: 59.6 us
  Pallas kernels  44.7 us (74%)
  local copies, waits for them, and re-layouts  14.8 us (25%)
    pallas_call x1, Pallas kernels, fused_shards(): pl.pallas_call(functools.partial(fused_kernel, dims), out_shape=jax.Shape...  44.7 us
    unnamed x9, local copies, waits for them, and re-layouts  14.2 us

profile of v1, /device:TPU:0, one launch (start us, length us, event | category | flops | bytes accessed | tf_op | source)
XLA Modules:
  0.0 59.6 jit_solution(15846059161104359106)
XLA Ops:
  0.0 0.0 copy-start.1
  0.0 0.0 copy-start.3
  0.0 0.0 copy-start.2
  0.0 0.0 copy-start
  0.0 14.2 %copy.6.cache_ref = bf16[4,2048,576]{2,1,0:T(8,128)(2,1)} copy(bf16[4,2048,576]{1,2,0:T(8,128)(2,1)} %param.6) | data formatting | bytes 18874368 | tf_op args[1]
  14.2 0.0 copy-done.1
  14.2 0.0 copy-done.3
  14.2 0.0 copy-done.2
  14.2 0.0 copy-done
  14.2 44.7 %shard_map.55 = f32[4,8,512]{2,1,0:T(8,128)S(1)} custom-call(s32[4]{0:T(128)S(1)} %copy-done.2, s32[4]{0:T(128)S(1)} %copy-done.3, bf16[2,4,16,576]{3,2,1,0:T(8,128)(2,1)S(1)} %bitcast.1, bf16[256,256]{1,0:T(8,128)(2,1)S(1)} %copy-done.1, bf16[4,2048,576]{2,1,0:T(8,128)(2,1)} %copy.6.cache_ref), custom_call_target="tpu_custom_call" | custom-call | tf_op jit(solution)/shard_map/pallas_call | solution.py:272
  58.9 0.6 %convert_element_type.7 = bf16[4,2,4,512]{3,2,1,0:T(4,128)(2,1)} reshape(bf16[4,8,512]{2,1,0:T(8,128)(2,1)S(1)} %convert_element_type.6) | data formatting | bytes 65536 | tf_op jit(solution)/shard_map/convert_element_type | solution.py:305
  (1 shorter events, 0.0 us)
Async XLA Ops:
  0.0 14.2 %copy-start.1 = (bf16[256,256]{1,0:T(8,128)(2,1)S(1)}, bf16[256,256]{1,0:T(8,128)(2,1)}, u32[]{:S(2)}) copy-start(bf16[256,256]{1,0:T(8,128)(2,1)} %constant.2.clone.order_ref) | copy-start | bytes 393220
  0.0 14.2 %copy-start.3 = (s32[4]{0:T(128)S(1)}, s32[4]{0:T(128)}, u32[]{:S(2)}) copy-start(s32[4]{0:T(128)} %owner_ref.1) | copy-start | bytes 52
  0.0 14.2 %copy-start.2 = (s32[4]{0:T(128)S(1)}, s32[4]{0:T(128)}, u32[]{:S(2)}) copy-start(s32[4]{0:T(128)} %lengths_ref.1) | copy-start | bytes 52
  0.0 14.2 %copy-start = (bf16[1,4,2,16,576]{4,3,2,1,0:T(8,128)(2,1)S(1)}, bf16[1,4,2,16,576]{4,3,2,1,0:T(8,128)(2,1)}, u32[]{:S(2)}) copy-start(bf16[1,4,2,16,576]{4,3,2,1,0:T(8,128)(2,1)} %param.5) | copy-start | bytes 442372

commit v2 on v1

--- a/solution.py
+++ b/solution.py
@@ -129,21 +129,32 @@
             pq(n, k).wait_recv()
             sq(n, k).start()
 
-    for n in range(chunks):
-        for k in range(1, groups):
-            zq(n, k).start()
+    for k in range(1, groups):
+        zq(0, k).start()
     for n in range(chunks):
         for k in range(1, groups):
             zq(n, k).wait_recv()
         for k in range(1, chips):
             pq(n, k).start()
         sq(n, 0).start()
-    forward(0)
+        if n + 1 < chunks:
+            for k in range(1, groups):
+                zq(n + 1, k).start()
+        if n == 0:
+            forward(0)
 
     blocks = groups * seqs
     rank = grp * seqs + seq
     stripe = slots // 2
     log_scale = softmax_scale * LOG2E
+
+    def plane_stage(at):
+        c_copy(at).wait_recv()
+        top, total, output = merge([packed[at, core], core_in[at]], latent)
+        plane_out[at, :, :, :latent] = output
+        plane_out[at, :, :, latent:] = pack_tail(top, total)
+        for k in range(1, chips):
+            p_copy(at, k).start()
 
     def step(b, carry):
         @pl.when(b < batch)
@@ -167,10 +178,12 @@
                     ).astype(jnp.bfloat16)
 
             cache_copy(b).wait()
-            scores = lax.dot_general(
-                query[...], cache[b], (((1,), (1,)), ((), ())),
-                preferred_element_type=jnp.float32,
-            )
+            scores = jnp.dot(query[...], cache[b], preferred_element_type=jnp.float32)
+
+            @pl.when(b >= 1)
+            def _():
+                plane_stage(b - 1)
+
             offset = lax.broadcasted_iota(jnp.int32, (1, slots), 1)
             position = jnp.where(
                 offset < stripe,
@@ -184,8 +197,8 @@
             top = jnp.maximum(jnp.max(scores, axis=1, keepdims=True), 0.1 * masked_score)
             weights = jnp.exp2((scores - top) * log_scale)
             total = jnp.sum(weights, axis=1, keepdims=True)
-            output = jnp.dot(
-                weights.astype(jnp.bfloat16), cache[b, :, :latent],
+            output = lax.dot_general(
+                weights.astype(jnp.bfloat16), cache[b, :latent], (((1,), (1,)), ((), ())),
                 preferred_element_type=jnp.float32,
             )
             split = (2, chips, groups * rows_per)
@@ -198,15 +211,9 @@
                 def _():
                     forward(n)
 
-        @pl.when((b >= 1) & (b < batch + 1))
+        @pl.when(b == batch)
         def _():
-            at = b - 1
-            c_copy(at).wait_recv()
-            top, total, output = merge([packed[at, core], core_in[at]], latent)
-            plane_out[at, :, :, :latent] = output
-            plane_out[at, :, :, latent:] = pack_tail(top, total)
-            for k in range(1, chips):
-                p_copy(at, k).start()
+            plane_stage(b - 1)
 
         @pl.when((b >= 2) & (b < batch + 2))
         def _():
@@ -282,7 +289,7 @@
         out_specs=pl.BlockSpec(memory_space=pltpu.VMEM),
         scratch_shapes=[pltpu.VMEM((seqs, groups, part_heads, width), bf16)] * chunks
         + [
-            pltpu.VMEM((batch, slots, width), bf16),
+            pltpu.VMEM((batch, width, slots), bf16),
             pltpu.VMEM((rows, width), bf16),
             pltpu.VMEM((batch, 2, chips, groups * rows_per, wide), f32),
             pltpu.VMEM((batch, chips, groups * rows_per, wide), f32),
@@ -301,7 +308,7 @@
         compiler_params=pltpu.CompilerParams(
             collective_id=0, has_side_effects=True, vmem_limit_bytes=48 * 1024 * 1024
         ),
-    )(lengths, owner_group, queries.reshape(chunks, groups, part_heads, width), order, latent_cache)
+    )(lengths, owner_group, queries.reshape(chunks, groups, part_heads, width), order, latent_cache.transpose(0, 2, 1))
     return out.reshape(batch, drafts, heads_per, latent).astype(bf16)
 
 

time: 60 us -> 46.2 us (0.77)
  local copies, waits for them, and re-layouts: 14.8 us -> 3.76 us
  Pallas kernels: 44.7 us -> 42.3 us
    unnamed x9 -> x8, local copies, waits for them, and re-layouts: 14.2 us -> 3.13 us
    pallas_call x1, Pallas kernels: 44.7 us -> 42.3 us  [fused_shards(): pl.pallas_call(functools.partial(fused_kernel, dims), out_shape=jax.Shape...]
where the time goes in v2:
time: 46.2 us; the launch traced here: 46.1 us
  Pallas kernels  42.3 us (92%)
  local copies, waits for them, and re-layouts  3.76 us (8%)
    pallas_call x1, Pallas kernels, fused_shards(): pl.pallas_call(functools.partial(fused_kernel, dims), out_shape=jax.Shape...  42.3 us
    unnamed x8, local copies, waits for them, and re-layouts  3.13 us

profile of v2, /device:TPU:0, one launch (start us, length us, event | category | flops | bytes accessed | tf_op | source)
XLA Modules:
  0.0 46.1 jit_solution(13351884604526289997)
XLA Ops:
  0.0 0.0 copy-start
  0.0 0.9 %copy-done = bf16[1,4,2,16,576]{4,3,2,1,0:T(8,128)(2,1)S(1)} copy-done((bf16[1,4,2,16,576]{4,3,2,1,0:T(8,128)(2,1)S(1)}, bf16[1,4,2,16,576]{4,3,2,1,0:T(8,128)(2,1)}, u32[]{:S(2)}) %copy-start) | copy-done | bytes 147480
  0.9 0.0 copy-start.1
  0.9 0.9 %copy-done.1 = bf16[256,256]{1,0:T(8,128)(2,1)S(1)} copy-done((bf16[256,256]{1,0:T(8,128)(2,1)S(1)}, bf16[256,256]{1,0:T(8,128)(2,1)}, u32[]{:S(2)}) %copy-start.1) | copy-done | bytes 131096
  1.8 0.0 copy-start.2
  1.8 0.7 %copy-done.2 = s32[4]{0:T(128)S(1)} copy-done((s32[4]{0:T(128)S(1)}, s32[4]{0:T(128)}, u32[]{:S(2)}) %copy-start.2) | copy-done | bytes 40
  2.5 0.0 copy-start.3
  2.5 0.7 %copy-done.3 = s32[4]{0:T(128)S(1)} copy-done((s32[4]{0:T(128)S(1)}, s32[4]{0:T(128)}, u32[]{:S(2)}) %copy-start.3) | copy-done | bytes 40
  3.1 42.3 %shard_map.55 = f32[4,8,512]{2,1,0:T(8,128)S(1)} custom-call(s32[4]{0:T(128)S(1)} %copy-done.2, s32[4]{0:T(128)S(1)} %copy-done.3, bf16[2,4,16,576]{3,2,1,0:T(8,128)(2,1)S(1)} %bitcast.2, bf16[256,256]{1,0:T(8,128)(2,1)S(1)} %copy-done.1, bf16[4,576,2048]{2,1,0:T(8,128)(2,1)} %bitcast.3), custom_call_target="tpu_custom_call" | custom-call | tf_op jit(solution)/shard_map/pallas_call | solution.py:279
  45.4 0.6 %convert_element_type.7 = bf16[4,2,4,512]{3,2,1,0:T(4,128)(2,1)} reshape(bf16[4,8,512]{2,1,0:T(8,128)(2,1)S(1)} %convert_element_type.6) | data formatting | bytes 65536 | tf_op jit(solution)/shard_map/convert_element_type | solution.py:312
  (1 shorter events, 0.0 us)
Async XLA Ops:
  0.0 0.9 %copy-start = (bf16[1,4,2,16,576]{4,3,2,1,0:T(8,128)(2,1)S(1)}, bf16[1,4,2,16,576]{4,3,2,1,0:T(8,128)(2,1)}, u32[]{:S(2)}) copy-start(bf16[1,4,2,16,576]{4,3,2,1,0:T(8,128)(2,1)} %param.5) | copy-start | bytes 442372
  0.9 0.9 %copy-start.1 = (bf16[256,256]{1,0:T(8,128)(2,1)S(1)}, bf16[256,256]{1,0:T(8,128)(2,1)}, u32[]{:S(2)}) copy-start(bf16[256,256]{1,0:T(8,128)(2,1)} %constant.2.clone.order_ref) | copy-start | bytes 393220
  1.8 0.7 %copy-start.2 = (s32[4]{0:T(128)S(1)}, s32[4]{0:T(128)}, u32[]{:S(2)}) copy-start(s32[4]{0:T(128)} %lengths_ref.1) | copy-start | bytes 52
  2.5 0.7 %copy-start.3 = (s32[4]{0:T(128)S(1)}, s32[4]{0:T(128)}, u32[]{:S(2)}) copy-start(s32[4]{0:T(128)} %owner_ref.1) | copy-start | bytes 52

commit v3 on v2

--- a/solution.py
+++ b/solution.py
@@ -46,14 +46,14 @@
     rows_per = drafts * heads_per
     rows = drafts * heads_per * groups * seqs
     gathered = scratch[:chunks]
-    (cache, query, packed, core_in, plane_out, plane_in, group_out, group_in) = scratch[
-        chunks : chunks + 8
-    ]
+    (
+        cache, query, packed, core_in, plane_out, tail_in, code_out, code_in, group_out, group_in,
+    ) = scratch[chunks : chunks + 10]
     (
         cache_sem,
         zq_send, zq_recv, pq_send, pq_recv, sq_send, sq_recv,
-        c_send, c_recv, p_send, p_recv, z_send, z_recv,
-    ) = scratch[chunks + 8 :]
+        c_send, c_recv, p_send, p_recv, t_send, t_recv, z_send, z_recv,
+    ) = scratch[chunks + 10 :]
 
     grp = lax.axis_index("grp")
     seq = lax.axis_index("seq")
@@ -114,8 +114,14 @@
 
     def p_copy(b, k):
         return remote(
-            plane_out.at[b, chip_peer(k)], plane_in.at[b, k - 1],
+            code_out.at[b, chip_peer(k)], code_in.at[b, k - 1],
             p_send.at[b, k - 1], p_recv.at[b, k - 1], (grp, chip_peer(k) * 2 + core),
+        )
+
+    def t_copy(b, k):
+        return remote(
+            plane_out.at[b, chip_peer(k), :, latent:], tail_in.at[b, k - 1],
+            t_send.at[b, k - 1], t_recv.at[b, k - 1], (grp, chip_peer(k) * 2 + core),
         )
 
     def z_copy(b, k):
@@ -152,8 +158,14 @@
         c_copy(at).wait_recv()
         top, total, output = merge([packed[at, core], core_in[at]], latent)
         plane_out[at, :, :, :latent] = output
-        plane_out[at, :, :, latent:] = pack_tail(top, total)
+        unit = jnp.max(jnp.abs(output), axis=-1, keepdims=True) * (1.0 / 32767.0)
+        unit = jnp.maximum(unit, 1e-37)
+        code_out[at] = jnp.round(output / unit).astype(jnp.int32).astype(jnp.int16)
+        tail = pack_tail(top, total)
+        lane = lax.broadcasted_iota(jnp.int32, tail.shape, 2)
+        plane_out[at, :, :, latent:] = jnp.where(lane == TAIL - 1, unit, tail)
         for k in range(1, chips):
+            t_copy(at, k).start()
             p_copy(at, k).start()
 
     def step(b, carry):
@@ -219,8 +231,13 @@
         def _():
             at = b - 2
             for k in range(1, chips):
+                t_copy(at, k).wait_recv()
                 p_copy(at, k).wait_recv()
-            parts = [plane_out[at, chip]] + [plane_in[at, k] for k in range(chips - 1)]
+            parts = [plane_out[at, chip]]
+            for k in range(chips - 1):
+                tail = tail_in[at, k]
+                values = code_in[at, k].astype(jnp.int32).astype(jnp.float32) * tail[:, TAIL - 1 :]
+                parts.append(jnp.concatenate([values, tail], axis=1))
             top, total, output = merge(parts, latent)
             group_out[at, :, :, :latent] = output.reshape(groups, rows_per, latent)
             group_out[at, :, :, latent:] = pack_tail(top, total).reshape(groups, rows_per, TAIL)
@@ -237,6 +254,7 @@
             out_ref[at] = output / total
             c_copy(at).wait_send()
             for k in range(1, chips):
+                t_copy(at, k).wait_send()
                 p_copy(at, k).wait_send()
             for k in range(1, groups):
                 z_copy(at, k).wait_send()
@@ -294,7 +312,9 @@
             pltpu.VMEM((batch, 2, chips, groups * rows_per, wide), f32),
             pltpu.VMEM((batch, chips, groups * rows_per, wide), f32),
             pltpu.VMEM((batch, chips, groups * rows_per, wide), f32),
-            pltpu.VMEM((batch, chips - 1, groups * rows_per, wide), f32),
+            pltpu.VMEM((batch, chips - 1, groups * rows_per, TAIL), f32),
+            pltpu.VMEM((batch, chips, groups * rows_per, latent), jnp.int16),
+            pltpu.VMEM((batch, chips - 1, groups * rows_per, latent), jnp.int16),
             pltpu.VMEM((batch, groups, rows_per, wide), f32),
             pltpu.VMEM((batch, groups - 1, rows_per, wide), f32),
             dma((batch,)),
@@ -302,6 +322,7 @@
             dma((chunks, chips - 1)), dma((chunks, chips - 1)),
             dma((chunks, chips)), dma((chunks, chips)),
             dma((batch,)), dma((batch,)),
+            dma((batch, chips - 1)), dma((batch, chips - 1)),
             dma((batch, chips - 1)), dma((batch, chips - 1)),
             dma((batch, groups - 1)), dma((batch, groups - 1)),
         ],

time: 46.2 us -> 44.6 us (0.965)
  Pallas kernels: 42.3 us -> 40.6 us
    pallas_call x1, Pallas kernels: 42.3 us -> 40.6 us  [fused_shards(): pl.pallas_call(functools.partial(fused_kernel, dims), out_shape=jax.Shape...]
where the time goes in v3:
time: 44.6 us; the launch traced here: 44.4 us
  Pallas kernels  40.6 us (91%)
  local copies, waits for them, and re-layouts  3.76 us (8%)
    pallas_call x1, Pallas kernels, fused_shards(): pl.pallas_call(functools.partial(fused_kernel, dims), out_shape=jax.Shape...  40.6 us
    unnamed x8, local copies, waits for them, and re-layouts  3.13 us

profile of v3, /device:TPU:0, one launch (start us, length us, event | category | flops | bytes accessed | tf_op | source)
XLA Modules:
  0.0 44.4 jit_solution(9612745427786231861)
XLA Ops:
  0.0 0.0 copy-start
  0.0 0.9 %copy-done = bf16[1,4,2,16,576]{4,3,2,1,0:T(8,128)(2,1)S(1)} copy-done((bf16[1,4,2,16,576]{4,3,2,1,0:T(8,128)(2,1)S(1)}, bf16[1,4,2,16,576]{4,3,2,1,0:T(8,128)(2,1)}, u32[]{:S(2)}) %copy-start) | copy-done | bytes 147480
  0.9 0.0 copy-start.1
  0.9 0.9 %copy-done.1 = bf16[256,256]{1,0:T(8,128)(2,1)S(1)} copy-done((bf16[256,256]{1,0:T(8,128)(2,1)S(1)}, bf16[256,256]{1,0:T(8,128)(2,1)}, u32[]{:S(2)}) %copy-start.1) | copy-done | bytes 131096
  1.8 0.0 copy-start.2
  1.8 0.7 %copy-done.2 = s32[4]{0:T(128)S(1)} copy-done((s32[4]{0:T(128)S(1)}, s32[4]{0:T(128)}, u32[]{:S(2)}) %copy-start.2) | copy-done | bytes 40
  2.5 0.0 copy-start.3
  2.5 0.7 %copy-done.3 = s32[4]{0:T(128)S(1)} copy-done((s32[4]{0:T(128)S(1)}, s32[4]{0:T(128)}, u32[]{:S(2)}) %copy-start.3) | copy-done | bytes 40
  3.1 40.6 %shard_map.55 = f32[4,8,512]{2,1,0:T(8,128)S(1)} custom-call(s32[4]{0:T(128)S(1)} %copy-done.2, s32[4]{0:T(128)S(1)} %copy-done.3, bf16[2,4,16,576]{3,2,1,0:T(8,128)(2,1)S(1)} %bitcast.2, bf16[256,256]{1,0:T(8,128)(2,1)S(1)} %copy-done.1, bf16[4,576,2048]{2,1,0:T(8,128)(2,1)} %bitcast.3), custom_call_target="tpu_custom_call" | custom-call | tf_op jit(solution)/shard_map/pallas_call | solution.py:297
  43.8 0.6 %convert_element_type.7 = bf16[4,2,4,512]{3,2,1,0:T(4,128)(2,1)} reshape(bf16[4,8,512]{2,1,0:T(8,128)(2,1)S(1)} %convert_element_type.6) | data formatting | bytes 65536 | tf_op jit(solution)/shard_map/convert_element_type | solution.py:333
  (1 shorter events, 0.0 us)
Async XLA Ops:
  0.0 0.9 %copy-start = (bf16[1,4,2,16,576]{4,3,2,1,0:T(8,128)(2,1)S(1)}, bf16[1,4,2,16,576]{4,3,2,1,0:T(8,128)(2,1)}, u32[]{:S(2)}) copy-start(bf16[1,4,2,16,576]{4,3,2,1,0:T(8,128)(2,1)} %param.5) | copy-start | bytes 442372
  0.9 0.9 %copy-start.1 = (bf16[256,256]{1,0:T(8,128)(2,1)S(1)}, bf16[256,256]{1,0:T(8,128)(2,1)}, u32[]{:S(2)}) copy-start(bf16[256,256]{1,0:T(8,128)(2,1)} %constant.2.clone.order_ref) | copy-start | bytes 393220
  1.8 0.7 %copy-start.2 = (s32[4]{0:T(128)S(1)}, s32[4]{0:T(128)}, u32[]{:S(2)}) copy-start(s32[4]{0:T(128)} %lengths_ref.1) | copy-start | bytes 52
  2.5 0.7 %copy-start.3 = (s32[4]{0:T(128)S(1)}, s32[4]{0:T(128)}, u32[]{:S(2)}) copy-start(s32[4]{0:T(128)} %owner_ref.1) | copy-start | bytes 52

commit v4 on v3

--- a/solution.py
+++ b/solution.py
@@ -70,9 +70,6 @@
     def cache_copy(b):
         return pltpu.make_async_copy(cache_ref.at[b], cache.at[b], cache_sem.at[b])
 
-    for b in range(batch):
-        cache_copy(b).start()
-
     peers = [(group_peer(k), seq) for k in range(1, groups)]
     peers += [(grp, chip_peer(k) * 2 + core) for k in range(1, chips)]
     peers += [(grp, sibling)]
@@ -80,6 +77,9 @@
     for peer in peers:
         pl.semaphore_signal(barrier, inc=1, device_id=peer, device_id_type=MESH)
 
+    for b in range(batch):
+        cache_copy(b).start()
+
     held = jnp.int32(0)
     for k in range(groups):
         held = jnp.where(owner_ref[k] == grp, k, held)
@@ -97,10 +97,11 @@
         ref = gathered[n].at[seq, grp]
         return remote(ref, ref, zq_send.at[n, k - 1], zq_recv.at[n, k - 1], (group_peer(k), seq))
 
-    def pq(n, k):
-        ref = gathered[n].at[seq]
+    def pq(n, k, j):
+        ref = gathered[n].at[seq, group_peer(groups - j)]
         return remote(
-            ref, ref, pq_send.at[n, k - 1], pq_recv.at[n, k - 1], (grp, chip_peer(k) * 2 + core)
+            ref, ref, pq_send.at[n, k - 1, j], pq_recv.at[n, k - 1, j],
+            (grp, chip_peer(k) * 2 + core),
         )
 
     def sq(n, k):
@@ -132,16 +133,18 @@
 
     def forward(n):
         for k in range(1, chips):
-            pq(n, k).wait_recv()
+            for j in range(groups):
+                pq(n, k, j).wait_recv()
             sq(n, k).start()
 
     for k in range(1, groups):
         zq(0, k).start()
     for n in range(chunks):
-        for k in range(1, groups):
-            zq(n, k).wait_recv()
-        for k in range(1, chips):
-            pq(n, k).start()
+        for j in range(groups):
+            if j:
+                zq(n, j).wait_recv()
+            for k in range(1, chips):
+                pq(n, k, j).start()
         sq(n, 0).start()
         if n + 1 < chunks:
             for k in range(1, groups):
@@ -266,7 +269,8 @@
         for k in range(1, groups):
             zq(n, k).wait_send()
         for k in range(1, chips):
-            pq(n, k).wait_send()
+            for j in range(groups):
+                pq(n, k, j).wait_send()
         for k in range(chips):
             sq(n, k).wait_send()
 
@@ -319,7 +323,7 @@
             pltpu.VMEM((batch, groups - 1, rows_per, wide), f32),
             dma((batch,)),
             dma((chunks, groups - 1)), dma((chunks, groups - 1)),
-            dma((chunks, chips - 1)), dma((chunks, chips - 1)),
+            dma((chunks, chips - 1, groups)), dma((chunks, chips - 1, groups)),
             dma((chunks, chips)), dma((chunks, chips)),
             dma((batch,)), dma((batch,)),
             dma((batch, chips - 1)), dma((batch, chips - 1)),

time: 44.6 us -> 43.7 us (0.980)
  Pallas kernels: 40.6 us -> 39.7 us
    pallas_call x1, Pallas kernels: 40.6 us -> 39.7 us  [fused_shards(): pl.pallas_call(functools.partial(fused_kernel, dims), out_shape=jax.Shape...]
where the time goes in v4:
time: 43.7 us; the launch traced here: 43.5 us
  Pallas kernels  39.7 us (91%)
  local copies, waits for them, and re-layouts  3.76 us (9%)
    pallas_call x1, Pallas kernels, fused_shards(): pl.pallas_call(functools.partial(fused_kernel, dims), out_shape=jax.Shape...  39.7 us
    unnamed x8, local copies, waits for them, and re-layouts  3.13 us

profile of v4, /device:TPU:0, one launch (start us, length us, event | category | flops | bytes accessed | tf_op | source)
XLA Modules:
  0.0 43.5 jit_solution(6818954343159661378)
XLA Ops:
  0.0 0.0 copy-start
  0.0 0.9 %copy-done = bf16[1,4,2,16,576]{4,3,2,1,0:T(8,128)(2,1)S(1)} copy-done((bf16[1,4,2,16,576]{4,3,2,1,0:T(8,128)(2,1)S(1)}, bf16[1,4,2,16,576]{4,3,2,1,0:T(8,128)(2,1)}, u32[]{:S(2)}) %copy-start) | copy-done | bytes 147480
  0.9 0.0 copy-start.1
  0.9 0.9 %copy-done.1 = bf16[256,256]{1,0:T(8,128)(2,1)S(1)} copy-done((bf16[256,256]{1,0:T(8,128)(2,1)S(1)}, bf16[256,256]{1,0:T(8,128)(2,1)}, u32[]{:S(2)}) %copy-start.1) | copy-done | bytes 131096
  1.8 0.0 copy-start.2
  1.8 0.7 %copy-done.2 = s32[4]{0:T(128)S(1)} copy-done((s32[4]{0:T(128)S(1)}, s32[4]{0:T(128)}, u32[]{:S(2)}) %copy-start.2) | copy-done | bytes 40
  2.5 0.0 copy-start.3
  2.5 0.7 %copy-done.3 = s32[4]{0:T(128)S(1)} copy-done((s32[4]{0:T(128)S(1)}, s32[4]{0:T(128)}, u32[]{:S(2)}) %copy-start.3) | copy-done | bytes 40
  3.1 39.7 %shard_map.55 = f32[4,8,512]{2,1,0:T(8,128)S(1)} custom-call(s32[4]{0:T(128)S(1)} %copy-done.2, s32[4]{0:T(128)S(1)} %copy-done.3, bf16[2,4,16,576]{3,2,1,0:T(8,128)(2,1)S(1)} %bitcast.2, bf16[256,256]{1,0:T(8,128)(2,1)S(1)} %copy-done.1, bf16[4,576,2048]{2,1,0:T(8,128)(2,1)} %bitcast.3), custom_call_target="tpu_custom_call" | custom-call | tf_op jit(solution)/shard_map/pallas_call | solution.py:301
  42.9 0.6 %convert_element_type.7 = bf16[4,2,4,512]{3,2,1,0:T(4,128)(2,1)} reshape(bf16[4,8,512]{2,1,0:T(8,128)(2,1)S(1)} %convert_element_type.6) | data formatting | bytes 65536 | tf_op jit(solution)/shard_map/convert_element_type | solution.py:337
  (1 shorter events, 0.0 us)
Async XLA Ops:
  0.0 0.9 %copy-start = (bf16[1,4,2,16,576]{4,3,2,1,0:T(8,128)(2,1)S(1)}, bf16[1,4,2,16,576]{4,3,2,1,0:T(8,128)(2,1)}, u32[]{:S(2)}) copy-start(bf16[1,4,2,16,576]{4,3,2,1,0:T(8,128)(2,1)} %param.5) | copy-start | bytes 442372
  0.9 0.9 %copy-start.1 = (bf16[256,256]{1,0:T(8,128)(2,1)S(1)}, bf16[256,256]{1,0:T(8,128)(2,1)}, u32[]{:S(2)}) copy-start(bf16[256,256]{1,0:T(8,128)(2,1)} %constant.2.clone.order_ref) | copy-start | bytes 393220
  1.8 0.7 %copy-start.2 = (s32[4]{0:T(128)S(1)}, s32[4]{0:T(128)}, u32[]{:S(2)}) copy-start(s32[4]{0:T(128)} %lengths_ref.1) | copy-start | bytes 52
  2.5 0.7 %copy-start.3 = (s32[4]{0:T(128)S(1)}, s32[4]{0:T(128)}, u32[]{:S(2)}) copy-start(s32[4]{0:T(128)} %owner_ref.1) | copy-start | bytes 52
